TPU v7x, 32 devices: a whole 2x2x4 slice. The times are simulated.
32 devices in a mesh: members: 2 (over x), tm: 16 (over z, y, core).
Axes of the slice: x: 2, y: 2, z: 4, core: 2. Of those that a mesh axis runs over, the one named last changes fastest.
Arguments:
- footprint: bfloat16 [8192, 128, 128], P(('members', 'tm')), parts along dimension 0, may hold values from -0.25 to 0.25
- block_row: int32 [32, 256], P(('members', 'tm')), parts along dimension 0, may hold values from 0 to 63
- block_col: int32 [32, 256], P(('members', 'tm')), parts along dimension 0, may hold values from 0 to 16383, as said below
- block_count: int32 [32], P(('members', 'tm')), parts along dimension 0, may hold values from 42 to 256, as said below
- observed_count: int32 [32], P(('members', 'tm')), parts along dimension 0, may hold values from 4096 to 8192, as said below
- emission: bfloat16 [32768, 128], P(('members', 'tm')), parts along dimension 0, may hold values from -6 to 6
- observed: float32 [2048, 128], P(('members', 'tm')), parts along dimension 0, may hold values from -6 to 6
- error_weight: float32 [2048, 128], P(('members', 'tm')), parts along dimension 0, may hold values from 0.25 to 4
- prior_precision: float32 [32768, 128], P(('members', 'tm')), parts along dimension 0, may hold values from 0.1 to 1
Outputs:
- gradient: float32 [32768, 128], P(('members', 'tm')), parts along dimension 0
- weighted_residual: float32 [2048, 128], P(('members', 'tm')), parts along dimension 0
There are 2 independent parts, one for each index of `members`. A program takes and returns all parts, laid end to end along the dimension named above; each array names one. Nothing has to cross between parts.
Inputs may be any that keep to these rules, and one draw needn't show every extreme that they name: The first block_count[s] slots of shard s are live, the rest are padding; some shard has all 256 slots live. `block_col`: among the live slots of one shard at most 16 name cell blocks of one region panel (1024 consecutive cell blocks); some panel receives exactly 16 from every shard. `observed_count`: some shard has all its observations valid.
All inputs are finite; a program needn't handle non-finite values.
Results may differ from a plain program's by a relative error of at most 0.0015.
Values may be sent and summed in bfloat16 or wider, within the bound.
A program may use at most 128 MiB of HBM per device.

v0:
```python
import math

import jax
import jax.numpy as jnp
from jax import lax
from jax.sharding import PartitionSpec as P


def on_device(
    footprint,
    block_row,
    block_col,
    block_count,
    observed_count,
    emission,
    observed,
    error_weight,
    prior_precision,
):
    slot_total = footprint.shape[0]
    block_width = footprint.shape[1]
    panel_blocks = emission.shape[0]
    obs_blocks = observed.shape[0]
    obs_block = block_row[0]
    cell_block = block_col[0]
    live_count = block_count[0]
    live_mask = jnp.arange(slot_total) < live_count
    group_size = math.gcd(64, slot_total)
    turn_total = (live_count + group_size - 1) // group_size
    all_panels = lax.all_gather(emission, "tm", axis=0, tiled=True)
    state_rows = all_panels[cell_block]

    def forward(step_index, obs_image):
        first_slot = step_index * group_size
        blocks = lax.dynamic_slice_in_dim(footprint, first_slot, group_size, 0)
        state_part = lax.dynamic_slice_in_dim(state_rows, first_slot, group_size, 0)
        keep_mask = lax.dynamic_slice_in_dim(live_mask, first_slot, group_size, 0)
        row_part = lax.dynamic_slice_in_dim(obs_block, first_slot, group_size, 0)
        products = jnp.einsum("kij,kj->ki", blocks, state_part, preferred_element_type=jnp.float32)
        products = jnp.where(keep_mask[:, None], products, 0.0)
        return obs_image + jax.ops.segment_sum(products, row_part, num_segments=obs_blocks)

    obs_image = lax.fori_loop(
        0, turn_total, forward, jnp.zeros((obs_blocks, block_width), jnp.float32)
    )
    obs_slot = jnp.arange(obs_blocks * block_width).reshape(obs_blocks, block_width)
    weighted = jnp.where(obs_slot < observed_count[0], error_weight * (obs_image - observed), 0.0)
    rounded = weighted.astype(jnp.bfloat16)
    residual_rows = rounded[obs_block]

    def adjoint(step_index, partials):
        first_slot = step_index * group_size
        blocks = lax.dynamic_slice_in_dim(footprint, first_slot, group_size, 0)
        residual_part = lax.dynamic_slice_in_dim(residual_rows, first_slot, group_size, 0)
        keep_mask = lax.dynamic_slice_in_dim(live_mask, first_slot, group_size, 0)
        products = jnp.einsum(
            "kij,ki->kj", blocks, residual_part, preferred_element_type=jnp.float32
        )
        products = jnp.where(keep_mask[:, None], products, 0.0)
        return lax.dynamic_update_slice_in_dim(partials, products, first_slot, 0)

    partials = lax.fori_loop(
        0, turn_total, adjoint, jnp.zeros((slot_total, block_width), jnp.float32)
    )
    in_range = live_mask & (cell_block >= 0) & (cell_block < panel_blocks * lax.axis_size("tm"))
    picked = jnp.where(in_range[:, None], partials, 0.0)
    summed = lax.psum_scatter(
        jax.ops.segment_sum(
            picked,
            jnp.where(in_range, cell_block, 0),
            num_segments=panel_blocks * lax.axis_size("tm"),
        ),
        "tm",
        scatter_dimension=0,
        tiled=True,
    )
    gradient = summed + prior_precision * emission.astype(jnp.float32)
    return (gradient, weighted)


def solution(mesh):
    placed = (
        P(("members", "tm"), None, None),
        P(("members", "tm"), None),
        P(("members", "tm"), None),
        P(("members", "tm")),
        P(("members", "tm")),
        P(("members", "tm"), None),
        P(("members", "tm"), None),
        P(("members", "tm"), None),
        P(("members", "tm"), None),
    )
    return jax.shard_map(
        on_device,
        mesh=mesh,
        in_specs=placed,
        out_specs=(P(("members", "tm"), None), P(("members", "tm"), None)),
        check_vma=False,
    )
```

profile of v0, /device:TPU:0, one launch (start us, length us, event | category | flops | bytes accessed | tf_op | source)
XLA Modules:
  0.0 213.9 jit_solution(14231270459999568873)
XLA Ops:
  7.2 0.0 copy-start.2
  7.2 0.0 copy-start.3
  7.2 0.0 all-gather.2.cloned.1.call-start
  7.2 0.7 all-gather.2.cloned.1.call-update
  7.9 0.0 reduce-scatter.2.cloned.1.call-start
  9.3 0.7 compare_select_fusion.1
  10.0 0.7 compare_select_fusion
  10.7 0.7 compare_reduce_fusion.1
  11.4 52.1 %all-gather.2.cloned.1.call-done = bf16[16384,128]{1,0:T(8,128)(2,1)} async-done(((bf16[1024,128]{1,0:T(8,128)(2,1)}), bf16[16384,128]{1,0:T(8,128)(2,1)}) %all-gather.2.cloned.1.call-update) | async-done | bytes 4194320 | tf_op jit(solution)/shard_map/all_gather | solution.py:30
  63.5 3.5 %gather_fusion = bf16[256,128]{1,0:T(8,128)(2,1)S(1)} fusion(bf16[16384,128]{1,0:T(8,128)(2,1)} %all-gather.2.cloned.1.call-done, s32[1024]{0:T(1024)S(1)} %pad_clamp_fusion.1), kind=kCustom, calls=%fused_computation | custom fusion | bytes 132096 | tf_op jit(solution)/shard_map/gather | solution.py:31
  66.9 9.3 %while.20 = (s32[]{:T(128)}, f32[64,128]{1,0:T(8,128)S(1)}, s32[]{:T(128)}, s32[256]{0:T(256)}, pred[256]{0:T(512)(128)(4,1)S(1)}, /*index=5*/bf16[256,128,128]{...) while((s32[]{:T(128)}, f32[64,128]{1,0:T(8,128)S(1)}, ...), condition=%wide.region_2.3_spmd, body=%wide.region_0.2_spmd.sunk | while | flops 2113542 | bytes 2245943 | solution.py:43
  67.0 0.1 dynamic_slice.37
  67.0 0.8 dynamic_slice.36
  67.8 2.8 %fusion.28 = f32[64,1,128]{2,1,0:T(1,128)S(1)} fusion(bf16[256,128,128]{2,1,0:T(8,128)(2,1)} %get-tuple-element.218, s32[]{:T(128)S(6)} %select_n.84, bf16[64,128,1]{1,0,2:T(8,128)(2,1)S(1)} %dynamic-slice_bitcast_fusion.4), kind=kOutput, calls=%fused_computation.10.clone.1 | convolution fusion | flops 2097152 | bytes 2146308 | tf_op jit(solution)/shard_map/while/body/kij,kj->ki/dot_general | solution.py:39
  70.5 1.0 scatter_custom_fusion.7
  71.6 0.1 dynamic_slice.37
  71.7 0.8 dynamic_slice.36
  72.4 2.8 %fusion.28 = f32[64,1,128]{2,1,0:T(1,128)S(1)} fusion(bf16[256,128,128]{2,1,0:T(8,128)(2,1)} %get-tuple-element.218, s32[]{:T(128)S(6)} %select_n.84, bf16[64,128,1]{1,0,2:T(8,128)(2,1)S(1)} %dynamic-slice_bitcast_fusion.4), kind=kOutput, calls=%fused_computation.10.clone.1 | convolution fusion | flops 2097152 | bytes 2146308 | tf_op jit(solution)/shard_map/while/body/kij,kj->ki/dot_general | solution.py:39
  75.2 1.0 scatter_custom_fusion.7
  76.2 0.0 copy-done.2
  76.2 0.0 copy-done.3
  76.2 0.6 fusion.17
  76.9 0.9 gather_fusion.1
  77.7 4.8 %while.21 = (s32[]{:T(128)}, f32[256,128]{1,0:T(8,128)S(1)}, s32[]{:T(128)}, pred[256]{0:T(512)(128)(4,1)S(1)}, bf16[256,128,128]{2,1,0:T(8,128)(2,1)}, /*index=...) while((s32[]{:T(128)}, f32[256,128]{1,0:T(8,128)S(1)}, s32[]{:T(128)}, ...), condition=%wide.region_4.5_spmd, body=%wide.region_3.4_spmd.sunk | while | flops 2105350 | bytes 2245411 | solution.py:62
  77.8 0.1 dynamic_slice.40
  77.9 2.2 %fusion.31 = f32[64,1,128]{2,1,0:T(1,128)S(1)} fusion(bf16[256,128,128]{2,1,0:T(8,128)(2,1)} %get-tuple-element.249, s32[]{:T(128)S(6)} %select_n.86, bf16[64,128,1]{1,0,2:T(8,128)(2,1)S(1)} %dynamic-slice_bitcast_fusion.5), kind=kOutput, calls=%fused_computation.4.clone.1 | convolution fusion | flops 2097152 | bytes 2146308 | tf_op jit(solution)/shard_map/while/body/kij,ki->kj/dot_general | solution.py:56
  80.1 0.1 select_dynamic-update-slice_fusion.2
  80.2 0.1 dynamic_slice.40
  80.3 2.2 %fusion.31 = f32[64,1,128]{2,1,0:T(1,128)S(1)} fusion(bf16[256,128,128]{2,1,0:T(8,128)(2,1)} %get-tuple-element.249, s32[]{:T(128)S(6)} %select_n.86, bf16[64,128,1]{1,0,2:T(8,128)(2,1)S(1)} %dynamic-slice_bitcast_fusion.5), kind=kOutput, calls=%fused_computation.4.clone.1 | convolution fusion | flops 2097152 | bytes 2146308 | tf_op jit(solution)/shard_map/while/body/kij,ki->kj/dot_general | solution.py:56
  82.5 0.1 select_dynamic-update-slice_fusion.2
  82.6 0.0 copy-start
  82.6 0.0 copy-start.1
  82.6 5.8 %scatter_custom_fusion.1 = f32[16384,128]{1,0:T(8,128)} fusion(s32[256]{0:T(256)S(1)} %bitcast.36, f32[]{:T(128)} %constant.29.clone.1, f32[256,128]{1,0:T(8,128)S(1)} %get-tuple-element.74, pred[256]{0:T(512)(128)(4,1)S(1)} %and_and_fusion), kind=kCustom, calls=%fused_computation.19 | custom fusion | flops 65536 | bytes 8521216 | tf_op jit(solution)/shard_map/scatter-add | solution.py:68
  88.4 0.0 reduce-scatter.2.cloned.1.call-update
  88.4 116.8 %reduce-scatter.2.cloned.1.call-done = f32[1024,128]{1,0:T(8,128)} async-done(((f32[16384,128]{1,0:T(8,128)}), f32[1024,128]{1,0:T(8,128)}) %reduce-scatter.2.cloned.1.call-update) | async-done | bytes 524304 | tf_op jit(solution)/shard_map/reduce_scatter | solution.py:67
  205.2 0.0 copy-done
  205.2 0.0 copy-done.1
  205.2 1.9 multiply_add_fusion
  (10 shorter events, 0.1 us)
Async XLA Ops:
  7.2 69.1 %copy-start.2 = (f32[64,128]{1,0:T(8,128)S(1)}, f32[64,128]{1,0:T(8,128)}, u32[]{:S(2)}) copy-start(f32[64,128]{1,0:T(8,128)} %param.20) | copy-start | bytes 98308
  7.2 69.1 %copy-start.3 = (f32[64,128]{1,0:T(8,128)S(1)}, f32[64,128]{1,0:T(8,128)}, u32[]{:S(2)}) copy-start(f32[64,128]{1,0:T(8,128)} %param.19) | copy-start | bytes 98308
  7.2 56.3 %all-gather.2.cloned.1.call-start = ((), (), s32[]{:S(2)}) async-start(), calls=%async_computation.1 | async-start | bytes 4456448 | tf_op jit(solution)/shard_map/all_gather | solution.py:30
  7.9 197.3 %reduce-scatter.2.cloned.1.call-start = ((), (), s32[]{:S(2)}) async-start(), calls=%async_computation.2 | async-start | bytes 8912896 | tf_op jit(solution)/shard_map/reduce_scatter | solution.py:67
  82.6 122.6 %copy-start = (bf16[1024,128]{1,0:T(8,128)(2,1)S(1)}, bf16[1024,128]{1,0:T(8,128)(2,1)}, u32[]{:S(2)}) copy-start(bf16[1024,128]{1,0:T(8,128)(2,1)} %param.18) | copy-start | bytes 786436
  82.6 122.6 %copy-start.1 = (f32[1024,128]{1,0:T(8,128)S(1)}, f32[1024,128]{1,0:T(8,128)}, u32[]{:S(2)}) copy-start(f32[1024,128]{1,0:T(8,128)} %param.21) | copy-start | bytes 1572868
Sparse Core Ops, SparseCore 0:
  10.2 53.2 all-gather.1
  88.5 116.6 reduce-scatter.1
where the time goes:
time: 214 us
  waiting for transfers between devices  170 us (79%)
  between operations  15.4 us (7%)
  other arithmetic  12.6 us (6%)
  matrix products  9.97 us (5%)
  local copies, waits for them, and re-layouts  6.2 us (3%)
    reduce_scatter x1, waiting for transfers between devices, on_device(): lax.psum_scatter(jax.ops.segment_sum(picked, jnp.where(in_range, cell_blo...  117 us
    all_gather x1, waiting for transfers between devices, on_device(): all_panels = lax.all_gather(emission, 'tm', axis=0, tiled=True)  52.1 us
    scatter-add x1, other arithmetic, on_device(): jax.ops.segment_sum(picked, jnp.where(in_range, cell_block, 0), num_segme...  5.78 us
    dot_general x2, matrix products, forward(): jnp.einsum('kij,kj->ki', blocks, state_part, preferred_element_type=jnp.f...  5.51 us
    dot_general x2, matrix products, adjoint(): jnp.einsum('kij,ki->kj', blocks, residual_part, preferred_element_type=jn...  4.46 us
  transfers between devices with their start and end apart: 2, of which 2 were waited for; matrix products, arithmetic and copies ran while one was open for 1% of the time, Pallas kernels for 0%

commit v1 on v0

v1 whole, which is shorter than its diff:
```python
import functools

import jax
import jax.numpy as jnp
from jax import lax
from jax.experimental import pallas as pl
from jax.experimental.pallas import tpu as pltpu
from jax.sharding import PartitionSpec as P

CAP = 16
GROUP = 8
CHUNKS = 8
MESH = pl.DeviceIdType.MESH
BF16 = jnp.bfloat16
F32 = jnp.float32
I32 = jnp.int32


def iota(shape, dim):
    return lax.broadcasted_iota(I32, shape, dim)


def nn(a, b):
    return lax.dot_general(a, b, (((1,), (0,)), ((), ())), preferred_element_type=F32)


def nt(a, b):
    return lax.dot_general(a, b, (((1,), (1,)), ((), ())), preferred_element_type=F32)


def to_column(row):
    m = row.shape[1]
    diagonal = iota((m, m), 0) == iota((m, m), 1)
    return jnp.sum(jnp.where(diagonal, row.astype(F32), 0.0), axis=1, keepdims=True).astype(I32)


def one_hot(mask):
    return jnp.where(mask, 1.0, 0.0).astype(BF16)


def split(value):
    high = value.astype(BF16)
    low = (value - high.astype(F32)).astype(BF16)
    return high, low


def kernel(
    n,
    foot_hbm,
    row_ref,
    col_ref,
    count_ref,
    valid_ref,
    emission_hbm,
    observed_hbm,
    weight_hbm,
    prior_hbm,
    gradient_ref,
    weighted_ref,
    foot,
    emission,
    observed,
    weight,
    prior,
    ask_send,
    ask_recv,
    x_send,
    x_recv,
    p_send,
    p_recv,
    state,
    image_rows,
    residual,
    partial,
    foot_sem,
    in_sem,
    ask_ssem,
    ask_rsem,
    x_ssem,
    x_rsem,
    p_ssem,
    p_rsem,
):
    me = lax.axis_index("tm")
    slots = foot.shape[0]
    width = foot.shape[1]
    panel = emission.shape[0]
    obs_blocks = observed.shape[0]
    places = n * CAP

    emission_copy = pltpu.make_async_copy(emission_hbm, emission, in_sem.at[0])
    observed_copy = pltpu.make_async_copy(observed_hbm, observed, in_sem.at[1])
    weight_copy = pltpu.make_async_copy(weight_hbm, weight, in_sem.at[2])
    prior_copy = pltpu.make_async_copy(prior_hbm, prior, in_sem.at[3])
    chunk = slots // CHUNKS
    foot_copies = [
        pltpu.make_async_copy(
            foot_hbm.at[pl.ds(c * chunk, chunk)], foot.at[pl.ds(c * chunk, chunk)], foot_sem.at[c]
        )
        for c in range(CHUNKS)
    ]
    emission_copy.start()
    barrier = pltpu.get_barrier_semaphore()

    @pl.loop(1, n)
    def _(d):
        pl.semaphore_signal(
            barrier, inc=1, device_id={"tm": lax.rem(me + d, n)}, device_id_type=MESH
        )

    for copy in foot_copies:
        copy.start()
    observed_copy.start()
    weight_copy.start()
    prior_copy.start()

    col = col_ref[...]
    live = iota((1, slots), 1) < count_ref[0]
    owner = lax.div(col, panel)
    local = col - owner * panel
    mine = (owner == iota((n, slots), 0)) & live
    before = one_hot(iota((slots, slots), 0) < iota((slots, slots), 1))
    rank_of = nn(one_hot(mine), before)
    rank = jnp.sum(jnp.where(mine, rank_of, 0.0), axis=0, keepdims=True).astype(I32)
    place = jnp.where(live, owner * CAP + rank, -1)

    wanted = local + 1
    high = lax.div(wanted, 32)
    low = wanted - high * 32
    asked = jnp.concatenate(
        [
            jnp.where(mine, high.astype(F32), 0.0),
            jnp.where(mine, low.astype(F32), 0.0),
        ],
        axis=0,
    ).astype(BF16)
    lane = jnp.where(live, me * CAP + rank, -1)
    spread = nt(asked, one_hot(iota((places, slots), 0) == lane))
    asks = spread[:n] * 32.0 + spread[n:]
    for p in range(n):
        ask_send[p] = asks[p : p + 1]
    ask_recv[me] = ask_send[me]

    pl.semaphore_wait(barrier, n - 1)

    def exchange(send, recv, ssem, rsem, view):
        def copy_to(d):
            peer = lax.rem(me + d, n)
            return pltpu.make_async_remote_copy(
                src_ref=view(send, peer),
                dst_ref=view(recv, me),
                send_sem=ssem.at[peer],
                recv_sem=rsem.at[me],
                device_id={"tm": peer},
                device_id_type=MESH,
            )

        def copy_from(d):
            peer = lax.rem(me + d, n)
            return pltpu.make_async_remote_copy(
                src_ref=view(send, peer),
                dst_ref=view(recv, peer),
                send_sem=ssem.at[peer],
                recv_sem=rsem.at[peer],
                device_id={"tm": peer},
                device_id_type=MESH,
            )

        def start():
            @pl.loop(1, n)
            def _(d):
                copy_to(d).start()

        def wait_recv():
            @pl.loop(1, n)
            def _(d):
                copy_from(d).wait_recv()

        def wait_send():
            @pl.loop(1, n)
            def _(d):
                copy_to(d).wait_send()

        return start, wait_recv, wait_send

    def one(ref, index):
        return ref.at[index]

    def rows(ref, index):
        return ref.at[pl.ds(pl.multiple_of(index * CAP, CAP), CAP)]

    own = pl.ds(pl.multiple_of(me * CAP, CAP), CAP)

    ask_start, ask_wait, ask_done = exchange(ask_send, ask_recv, ask_ssem, ask_rsem, one)
    x_start, x_wait, x_done = exchange(x_send, x_recv, x_ssem, x_rsem, rows)
    p_start, p_wait, p_done = exchange(p_send, p_recv, p_ssem, p_rsem, rows)

    ask_start()
    place_column = to_column(place)
    to_slot = one_hot(place_column == iota((slots, places), 1))
    obs_row = jnp.where(live, row_ref[...], -1)
    obs_column = to_column(obs_row)
    emission_copy.wait()
    ask_wait()

    total = jnp.sum(ask_recv[...], axis=0).astype(I32)
    picked = nn(one_hot(to_column(total) == iota((places, panel), 1) + 1), emission[...])
    x_send[...] = picked.astype(BF16)
    x_recv[own] = x_send[own]
    x_start()

    for copy in foot_copies:
        copy.wait()
    observed_copy.wait()
    weight_copy.wait()
    x_wait()

    state[...] = nn(to_slot, x_recv[...])

    sub = iota((GROUP, width), 0)

    @pl.loop(0, slots // GROUP, unroll=8)
    def _(g):
        at = pl.ds(pl.multiple_of(g * GROUP, GROUP), GROUP)
        blocks = foot[at].reshape(GROUP * width, width)
        product = nt(state[at].astype(BF16), blocks)
        out = jnp.zeros((GROUP, width), F32)
        for k in range(GROUP):
            out = jnp.where(sub == k, product[:, k * width : (k + 1) * width], out)
        image_rows[at] = out

    to_obs = one_hot(obs_row == iota((obs_blocks, slots), 0))
    rows_value = image_rows[...]
    high, low = split(rows_value)
    image = nn(to_obs, high) + nn(to_obs, low)
    obs_slot = iota((obs_blocks, width), 0) * width + iota((obs_blocks, width), 1)
    misfit = jnp.where(obs_slot < valid_ref[0], weight[...] * (image - observed[...]), 0.0)
    weighted_ref[...] = misfit
    residual[...] = nn(one_hot(obs_column == iota((slots, obs_blocks), 1)), misfit.astype(BF16))

    @pl.loop(0, slots // GROUP, unroll=8)
    def _(g):
        at = pl.ds(pl.multiple_of(g * GROUP, GROUP), GROUP)
        blocks = foot[at].reshape(GROUP * width, width)
        value = residual[at]
        spread_out = jnp.concatenate(
            [jnp.where(sub == k, value, 0.0) for k in range(GROUP)], axis=1
        ).astype(BF16)
        partial[at] = nn(spread_out, blocks)

    high, low = split(partial[...])
    to_place = one_hot(iota((places, slots), 0) == place)
    p_send[:, :width] = nn(to_place, high).astype(BF16)
    p_send[:, width:] = nn(to_place, low).astype(BF16)
    p_recv[own] = p_send[own]
    p_start()
    scatter = one_hot(iota((panel, places), 0) + 1 == total)
    prior_copy.wait()
    ask_done()
    x_done()
    p_wait()
    summed = nn(scatter, p_recv[...])
    gradient_ref[...] = (
        summed[:, :width] + summed[:, width:] + prior[...] * emission[...].astype(F32)
    )
    p_done()


def on_device(
    footprint,
    block_row,
    block_col,
    block_count,
    observed_count,
    emission,
    observed,
    error_weight,
    prior_precision,
):
    n = lax.axis_size("tm")
    slots, width, _ = footprint.shape
    panel = emission.shape[0]
    obs_blocks = observed.shape[0]
    places = n * CAP
    any_spec = pl.BlockSpec(memory_space=pl.ANY)
    vmem_spec = pl.BlockSpec(memory_space=pltpu.VMEM)
    smem_spec = pl.BlockSpec(memory_space=pltpu.SMEM)
    dma = pltpu.SemaphoreType.DMA
    return pl.pallas_call(
        functools.partial(kernel, n),
        out_shape=(
            jax.ShapeDtypeStruct((panel, width), F32),
            jax.ShapeDtypeStruct((obs_blocks, width), F32),
        ),
        in_specs=[
            any_spec,
            vmem_spec,
            vmem_spec,
            smem_spec,
            smem_spec,
            any_spec,
            any_spec,
            any_spec,
            any_spec,
        ],
        out_specs=(vmem_spec, vmem_spec),
        scratch_shapes=[
            pltpu.VMEM((slots, width, width), BF16),
            pltpu.VMEM((panel, width), BF16),
            pltpu.VMEM((obs_blocks, width), F32),
            pltpu.VMEM((obs_blocks, width), F32),
            pltpu.VMEM((panel, width), F32),
            pltpu.VMEM((n, 1, places), F32),
            pltpu.VMEM((n, 1, places), F32),
            pltpu.VMEM((places, width), BF16),
            pltpu.VMEM((places, width), BF16),
            pltpu.VMEM((places, 2 * width), BF16),
            pltpu.VMEM((places, 2 * width), BF16),
            pltpu.VMEM((slots, width), F32),
            pltpu.VMEM((slots, width), F32),
            pltpu.VMEM((slots, width), F32),
            pltpu.VMEM((slots, width), F32),
            dma((CHUNKS,)),
            dma((4,)),
            dma((n,)),
            dma((n,)),
            dma((n,)),
            dma((n,)),
            dma((n,)),
            dma((n,)),
        ],
        compiler_params=pltpu.CompilerParams(
            collective_id=0, has_side_effects=True, vmem_limit_bytes=48 * 1024 * 1024
        ),
        cost_estimate=pl.CostEstimate(
            flops=4 * slots * width * width,
            bytes_accessed=footprint.size * 2 + panel * width * 10,
            transcendentals=0,
        ),
    )(
        footprint,
        block_row,
        block_col,
        block_count,
        observed_count,
        emission,
        observed,
        error_weight,
        prior_precision,
    )


def solution(mesh):
    placed = (
        P(("members", "tm"), None, None),
        P(("members", "tm"), None),
        P(("members", "tm"), None),
        P(("members", "tm")),
        P(("members", "tm")),
        P(("members", "tm"), None),
        P(("members", "tm"), None),
        P(("members", "tm"), None),
        P(("members", "tm"), None),
    )
    return jax.shard_map(
        on_device,
        mesh=mesh,
        in_specs=placed,
        out_specs=(P(("members", "tm"), None), P(("members", "tm"), None)),
        check_vma=False,
    )
```

time: 214 us -> 33 us (0.15)
  waiting for transfers between devices: 170 us -> 0 us
  Pallas kernels: 0 us -> 24.4 us
  between operations: 15.4 us -> 1.95 us
  other arithmetic: 12.6 us -> 0 us
  matrix products: 9.97 us -> 0 us
    reduce_scatter x1 -> x0, waiting for transfers between devices: 117 us -> none  [on_device(): lax.psum_scatter(jax.ops.segment_sum(picked, jnp.where(in_range, cell_blo...]
    all_gather x1 -> x0, waiting for transfers between devices: 52.1 us -> none  [on_device(): all_panels = lax.all_gather(emission, 'tm', axis=0, tiled=True)]
    pallas_call x0 -> x1, Pallas kernels: none -> 24.4 us  [on_device(): pl.pallas_call(functools.partial(kernel, n), out_shape=(jax.ShapeDtypeStr...]
    dot_general x4 -> x0, matrix products: 9.97 us -> none  [the longest x2 5.51 us: forward(): jnp.einsum('kij,kj->ki', blocks, state_part, preferred_element_type=jnp.f...]
    scatter-add x3 -> x0, other arithmetic: 7.83 us -> none  [the longest x1 5.78 us: on_device(): jax.ops.segment_sum(picked, jnp.where(in_range, cell_block, 0), num_segme...]
    unnamed x8 -> x14, local copies, waits for them, and re-layouts: 0.04 us -> 6.27 us
    gather x2 -> x0, local copies, waits for them, and re-layouts: 4.31 us -> none  [the longest x1 3.45 us: on_device(): state_rows = all_panels[cell_block]]
  transfers between devices with their start and end apart: 2 -> 0, of which waited for: 2 -> 0; matrix products, arithmetic and copies ran while one was open for 1% -> 0% of each run, Pallas kernels for 0% -> 0%
where the time goes in v1:
time: 33 us; the launch traced here: 32.7 us
  Pallas kernels  24.4 us (74%)
  local copies, waits for them, and re-layouts  6.27 us (19%)
  between operations  1.95 us (6%)
    pallas_call x1, Pallas kernels, on_device(): pl.pallas_call(functools.partial(kernel, n), out_shape=(jax.ShapeDtypeStr...  24.4 us
    unnamed x14, local copies, waits for them, and re-layouts  6.27 us

profile of v1, /device:TPU:0, one launch (start us, length us, event | category | flops | bytes accessed | tf_op | source)
XLA Modules:
  0.0 32.7 jit_solution(11732677616079623254)
XLA Ops:
  1.9 0.0 copy-start
  1.9 1.0 %copy-done = f32[1024,128]{1,0:T(8,128)S(1)} copy-done((f32[1024,128]{1,0:T(8,128)S(1)}, f32[1024,128]{1,0:T(8,128)}, u32[]{:S(2)}) %copy-start) | copy-done | bytes 524312
  3.0 0.0 copy-start.1
  3.0 0.9 %copy-done.1 = bf16[1024,128]{1,0:T(8,128)(2,1)S(1)} copy-done((bf16[1024,128]{1,0:T(8,128)(2,1)S(1)}, bf16[1024,128]{1,0:T(8,128)(2,1)}, u32[]{:S(2)}) %copy-start.1) | copy-done | bytes 262168
  3.9 0.0 copy-start.2
  3.9 0.8 %copy-done.2 = f32[64,128]{1,0:T(8,128)S(1)} copy-done((f32[64,128]{1,0:T(8,128)S(1)}, f32[64,128]{1,0:T(8,128)}, u32[]{:S(2)}) %copy-start.2) | copy-done | bytes 32792
  4.7 0.0 copy-start.3
  4.7 0.8 %copy-done.3 = f32[64,128]{1,0:T(8,128)S(1)} copy-done((f32[64,128]{1,0:T(8,128)S(1)}, f32[64,128]{1,0:T(8,128)}, u32[]{:S(2)}) %copy-start.3) | copy-done | bytes 32792
  5.4 0.0 copy-start.4
  5.4 0.7 %copy-done.4 = s32[1,256]{1,0:T(1,128)S(1)} copy-done((s32[1,256]{1,0:T(1,128)S(1)}, s32[1,256]{1,0:T(1,128)}, u32[]{:S(2)}) %copy-start.4) | copy-done | bytes 1048
  6.1 0.0 copy-start.5
  6.1 0.7 %copy-done.5 = s32[1,256]{1,0:T(1,128)S(1)} copy-done((s32[1,256]{1,0:T(1,128)S(1)}, s32[1,256]{1,0:T(1,128)}, u32[]{:S(2)}) %copy-start.5) | copy-done | bytes 1048
  6.8 24.4 %shard_map.104 = (f32[1024,128]{1,0:T(8,128)S(1)}, f32[64,128]{1,0:T(8,128)S(1)}) custom-call(bf16[256,128,128]{2,1,0:T(8,128)(2,1)} %foot_hbm.1, s32[1,256]{1,0:T(1,128)S(1)} %copy-done.4, s32[1,256]{1,0:T(1,128)S(1)} %copy-done.5, s32[1]{0:T(128)S(6)} %copy.13.count_ref, s32[1]{0:T(128)S(6)} %copy.14.valid_ref, bf16[1024,128]{1,0:T(8,128)(2,1)S(1)} %copy-done.1, ...), custom_call_target="tpu_custom_call" | custom-call | flops 16777216 | bytes 9699328 | tf_op jit(solution)/shard_map/pallas_call | solution.py:289
  31.2 0.8 %copy.15 = f32[1024,128]{1,0:T(8,128)} copy(f32[1024,128]{1,0:T(8,128)S(1)} %get-tuple-element.4) | data formatting | bytes 1048576
  32.0 0.6 %copy.16 = f32[64,128]{1,0:T(8,128)} copy(f32[64,128]{1,0:T(8,128)S(1)} %get-tuple-element.5) | data formatting | bytes 65536
Async XLA Ops:
  1.9 1.0 %copy-start = (f32[1024,128]{1,0:T(8,128)S(1)}, f32[1024,128]{1,0:T(8,128)}, u32[]{:S(2)}) copy-start(f32[1024,128]{1,0:T(8,128)} %prior_hbm.1) | copy-start | bytes 1572868
  3.0 0.9 %copy-start.1 = (bf16[1024,128]{1,0:T(8,128)(2,1)S(1)}, bf16[1024,128]{1,0:T(8,128)(2,1)}, u32[]{:S(2)}) copy-start(bf16[1024,128]{1,0:T(8,128)(2,1)} %emission_hbm.1) | copy-start | bytes 786436
  3.9 0.8 %copy-start.2 = (f32[64,128]{1,0:T(8,128)S(1)}, f32[64,128]{1,0:T(8,128)}, u32[]{:S(2)}) copy-start(f32[64,128]{1,0:T(8,128)} %observed_hbm.1) | copy-start | bytes 98308
  4.7 0.8 %copy-start.3 = (f32[64,128]{1,0:T(8,128)S(1)}, f32[64,128]{1,0:T(8,128)}, u32[]{:S(2)}) copy-start(f32[64,128]{1,0:T(8,128)} %weight_hbm.1) | copy-start | bytes 98308
  5.4 0.7 %copy-start.4 = (s32[1,256]{1,0:T(1,128)S(1)}, s32[1,256]{1,0:T(1,128)}, u32[]{:S(2)}) copy-start(s32[1,256]{1,0:T(1,128)} %row_ref.1) | copy-start | bytes 3076
  6.1 0.7 %copy-start.5 = (s32[1,256]{1,0:T(1,128)S(1)}, s32[1,256]{1,0:T(1,128)}, u32[]{:S(2)}) copy-start(s32[1,256]{1,0:T(1,128)} %col_ref.1) | copy-start | bytes 3076

commit v2 on v1

--- a/solution.py
+++ b/solution.py
@@ -47,16 +47,20 @@
 def kernel(
     n,
     foot_hbm,
-    row_ref,
-    col_ref,
-    count_ref,
-    valid_ref,
+    row_hbm,
+    col_hbm,
+    count_hbm,
+    valid_hbm,
     emission_hbm,
     observed_hbm,
     weight_hbm,
     prior_hbm,
     gradient_ref,
     weighted_ref,
+    row_ref,
+    col_ref,
+    count_ref,
+    valid_ref,
     foot,
     emission,
     observed,
@@ -88,6 +92,12 @@
     obs_blocks = observed.shape[0]
     places = n * CAP
 
+    col_copy = pltpu.make_async_copy(col_hbm, col_ref, in_sem.at[4])
+    count_copy = pltpu.make_async_copy(count_hbm, count_ref, in_sem.at[5])
+    row_copy = pltpu.make_async_copy(row_hbm, row_ref, in_sem.at[6])
+    valid_copy = pltpu.make_async_copy(valid_hbm, valid_ref, in_sem.at[7])
+    col_copy.start()
+    count_copy.start()
     emission_copy = pltpu.make_async_copy(emission_hbm, emission, in_sem.at[0])
     observed_copy = pltpu.make_async_copy(observed_hbm, observed, in_sem.at[1])
     weight_copy = pltpu.make_async_copy(weight_hbm, weight, in_sem.at[2])
@@ -99,7 +109,6 @@
         )
         for c in range(CHUNKS)
     ]
-    emission_copy.start()
     barrier = pltpu.get_barrier_semaphore()
 
     @pl.loop(1, n)
@@ -108,11 +117,16 @@
             barrier, inc=1, device_id={"tm": lax.rem(me + d, n)}, device_id_type=MESH
         )
 
+    row_copy.start()
+    emission_copy.start()
+    valid_copy.start()
     for copy in foot_copies:
         copy.start()
     observed_copy.start()
     weight_copy.start()
     prior_copy.start()
+    col_copy.wait()
+    count_copy.wait()
 
     col = col_ref[...]
     live = iota((1, slots), 1) < count_ref[0]
@@ -156,7 +170,7 @@
             )
 
         def copy_from(d):
-            peer = lax.rem(me + d, n)
+            peer = lax.rem(me - d + n, n)
             return pltpu.make_async_remote_copy(
                 src_ref=view(send, peer),
                 dst_ref=view(recv, peer),
@@ -198,6 +212,7 @@
     ask_start()
     place_column = to_column(place)
     to_slot = one_hot(place_column == iota((slots, places), 1))
+    row_copy.wait()
     obs_row = jnp.where(live, row_ref[...], -1)
     obs_column = to_column(obs_row)
     emission_copy.wait()
@@ -213,13 +228,14 @@
         copy.wait()
     observed_copy.wait()
     weight_copy.wait()
+    valid_copy.wait()
     x_wait()
 
     state[...] = nn(to_slot, x_recv[...])
 
     sub = iota((GROUP, width), 0)
 
-    @pl.loop(0, slots // GROUP, unroll=8)
+    @pl.loop(0, slots // GROUP, unroll=32)
     def _(g):
         at = pl.ds(pl.multiple_of(g * GROUP, GROUP), GROUP)
         blocks = foot[at].reshape(GROUP * width, width)
@@ -238,7 +254,7 @@
     weighted_ref[...] = misfit
     residual[...] = nn(one_hot(obs_column == iota((slots, obs_blocks), 1)), misfit.astype(BF16))
 
-    @pl.loop(0, slots // GROUP, unroll=8)
+    @pl.loop(0, slots // GROUP, unroll=32)
     def _(g):
         at = pl.ds(pl.multiple_of(g * GROUP, GROUP), GROUP)
         blocks = foot[at].reshape(GROUP * width, width)
@@ -264,6 +280,10 @@
         summed[:, :width] + summed[:, width:] + prior[...] * emission[...].astype(F32)
     )
     p_done()
+
+
+def in_hbm(value):
+    return pltpu.with_memory_space_constraint(value, pltpu.HBM)
 
 
 def on_device(
@@ -282,29 +302,24 @@
     panel = emission.shape[0]
     obs_blocks = observed.shape[0]
     places = n * CAP
+    hbm_spec = pl.BlockSpec(memory_space=pltpu.HBM)
     any_spec = pl.BlockSpec(memory_space=pl.ANY)
     vmem_spec = pl.BlockSpec(memory_space=pltpu.VMEM)
-    smem_spec = pl.BlockSpec(memory_space=pltpu.SMEM)
     dma = pltpu.SemaphoreType.DMA
-    return pl.pallas_call(
+    outs = (
+        jax.ShapeDtypeStruct((panel, width), F32),
+        jax.ShapeDtypeStruct((obs_blocks, width), F32),
+    )
+    results = pl.pallas_call(
         functools.partial(kernel, n),
-        out_shape=(
-            jax.ShapeDtypeStruct((panel, width), F32),
-            jax.ShapeDtypeStruct((obs_blocks, width), F32),
-        ),
-        in_specs=[
-            any_spec,
-            vmem_spec,
-            vmem_spec,
-            smem_spec,
-            smem_spec,
-            any_spec,
-            any_spec,
-            any_spec,
-            any_spec,
-        ],
+        out_shape=outs,
+        in_specs=[hbm_spec] * 9,
         out_specs=(vmem_spec, vmem_spec),
         scratch_shapes=[
+            pltpu.VMEM((1, slots), I32),
+            pltpu.VMEM((1, slots), I32),
+            pltpu.SMEM((1,), I32),
+            pltpu.SMEM((1,), I32),
             pltpu.VMEM((slots, width, width), BF16),
             pltpu.VMEM((panel, width), BF16),
             pltpu.VMEM((obs_blocks, width), F32),
@@ -321,7 +336,7 @@
             pltpu.VMEM((slots, width), F32),
             pltpu.VMEM((slots, width), F32),
             dma((CHUNKS,)),
-            dma((4,)),
+            dma((8,)),
             dma((n,)),
             dma((n,)),
             dma((n,)),
@@ -338,16 +353,17 @@
             transcendentals=0,
         ),
     )(
-        footprint,
-        block_row,
-        block_col,
+        in_hbm(footprint),
+        in_hbm(block_row),
+        in_hbm(block_col),
         block_count,
         observed_count,
-        emission,
-        observed,
-        error_weight,
-        prior_precision,
-    )
+        in_hbm(emission),
+        in_hbm(observed),
+        in_hbm(error_weight),
+        in_hbm(prior_precision),
+    )
+    return results
 
 
 def solution(mesh):

time: 33 us -> 27.3 us (0.83)
  local copies, waits for them, and re-layouts: 6.27 us -> 1.41 us
  Pallas kernels: 24.4 us -> 23.8 us
    unnamed x14 -> x2, local copies, waits for them, and re-layouts: 6.27 us -> 1.41 us
    pallas_call x1, Pallas kernels: 24.4 us -> 23.8 us  [on_device(): pl.pallas_call(functools.partial(kernel, n), out_shape=outs, in_specs=[hb...]
where the time goes in v2:
time: 27.3 us; the launch traced here: 27.1 us
  Pallas kernels  23.8 us (87%)
  between operations  1.93 us (7%)
  local copies, waits for them, and re-layouts  1.41 us (5%)
    pallas_call x1, Pallas kernels, on_device(): pl.pallas_call(functools.partial(kernel, n), out_shape=outs, in_specs=[hb...  23.8 us
    unnamed x2, local copies, waits for them, and re-layouts  1.41 us

profile of v2, /device:TPU:0, one launch (start us, length us, event | category | flops | bytes accessed | tf_op | source)
XLA Modules:
  0.0 27.1 jit_solution(17226493962408999624)
XLA Ops:
  1.9 23.8 %shard_map.104 = (f32[1024,128]{1,0:T(8,128)S(1)}, f32[64,128]{1,0:T(8,128)S(1)}) custom-call(bf16[256,128,128]{2,1,0:T(8,128)(2,1)} %foot_hbm.1, s32[1,256]{1,0:T(1,128)} %row_hbm.1, s32[1,256]{1,0:T(1,128)} %col_hbm.1, s32[1]{0:T(128)S(6)} %copy.13.count_hbm, s32[1]{0:T(128)S(6)} %copy.14.valid_hbm, bf16[1024,128]{1,0:T(8,128)(2,1)} %emission_hbm.1, ...), custom_call_target="tpu_custom_call" | custom-call | flops 16777216 | bytes 9699328 | tf_op jit(solution)/shard_map/pallas_call | solution.py:313
  25.7 0.8 %copy.15 = f32[1024,128]{1,0:T(8,128)} copy(f32[1024,128]{1,0:T(8,128)S(1)} %get-tuple-element.4) | data formatting | bytes 1048576
  26.5 0.6 %copy.16 = f32[64,128]{1,0:T(8,128)} copy(f32[64,128]{1,0:T(8,128)S(1)} %get-tuple-element.5) | data formatting | bytes 65536

commit v3 on v2

--- a/solution.py
+++ b/solution.py
@@ -8,7 +8,7 @@
 from jax.sharding import PartitionSpec as P
 
 CAP = 16
-GROUP = 8
+BATCH = 4
 CHUNKS = 8
 MESH = pl.DeviceIdType.MESH
 BF16 = jnp.bfloat16
@@ -72,11 +72,12 @@
     x_recv,
     p_send,
     p_recv,
-    state,
+    slot_row,
+    slot_at,
     image_rows,
     residual,
-    partial,
     foot_sem,
+    slot_sem,
     in_sem,
     ask_ssem,
     ask_rsem,
@@ -157,129 +158,147 @@
 
     pl.semaphore_wait(barrier, n - 1)
 
-    def exchange(send, recv, ssem, rsem, view):
-        def copy_to(d):
-            peer = lax.rem(me + d, n)
-            return pltpu.make_async_remote_copy(
-                src_ref=view(send, peer),
-                dst_ref=view(recv, me),
-                send_sem=ssem.at[peer],
-                recv_sem=rsem.at[me],
-                device_id={"tm": peer},
-                device_id_type=MESH,
-            )
-
-        def copy_from(d):
-            peer = lax.rem(me - d + n, n)
-            return pltpu.make_async_remote_copy(
-                src_ref=view(send, peer),
-                dst_ref=view(recv, peer),
-                send_sem=ssem.at[peer],
-                recv_sem=rsem.at[peer],
-                device_id={"tm": peer},
-                device_id_type=MESH,
-            )
-
-        def start():
-            @pl.loop(1, n)
-            def _(d):
-                copy_to(d).start()
-
-        def wait_recv():
-            @pl.loop(1, n)
-            def _(d):
-                copy_from(d).wait_recv()
-
-        def wait_send():
-            @pl.loop(1, n)
-            def _(d):
-                copy_to(d).wait_send()
-
-        return start, wait_recv, wait_send
+    def copy_to(exchange, d):
+        send, recv, ssem, rsem, view = exchange
+        peer = lax.rem(me + d, n)
+        return pltpu.make_async_remote_copy(
+            src_ref=view(send, peer),
+            dst_ref=view(recv, me),
+            send_sem=ssem.at[peer],
+            recv_sem=rsem.at[me],
+            device_id={"tm": peer},
+            device_id_type=MESH,
+        )
+
+    def copy_from(exchange, d):
+        send, recv, ssem, rsem, view = exchange
+        peer = lax.rem(me - d + n, n)
+        return pltpu.make_async_remote_copy(
+            src_ref=view(send, peer),
+            dst_ref=view(recv, peer),
+            send_sem=ssem.at[peer],
+            recv_sem=rsem.at[peer],
+            device_id={"tm": peer},
+            device_id_type=MESH,
+        )
+
+    def start(exchange):
+        @pl.loop(1, n)
+        def _(d):
+            copy_to(exchange, d).start()
+
+    def wait_recv(exchange):
+        @pl.loop(1, n)
+        def _(d):
+            copy_from(exchange, d).wait_recv()
+
+    def wait_send(exchange):
+        @pl.loop(1, n)
+        def _(d):
+            copy_to(exchange, d).wait_send()
 
     def one(ref, index):
         return ref.at[index]
 
+    def span(index):
+        return pl.ds(pl.multiple_of(index * CAP, CAP), CAP)
+
     def rows(ref, index):
-        return ref.at[pl.ds(pl.multiple_of(index * CAP, CAP), CAP)]
-
-    own = pl.ds(pl.multiple_of(me * CAP, CAP), CAP)
-
-    ask_start, ask_wait, ask_done = exchange(ask_send, ask_recv, ask_ssem, ask_rsem, one)
-    x_start, x_wait, x_done = exchange(x_send, x_recv, x_ssem, x_rsem, rows)
-    p_start, p_wait, p_done = exchange(p_send, p_recv, p_ssem, p_rsem, rows)
-
-    ask_start()
-    place_column = to_column(place)
-    to_slot = one_hot(place_column == iota((slots, places), 1))
+        return ref.at[span(index)]
+
+    own = span(me)
+    ask = (ask_send, ask_recv, ask_ssem, ask_rsem, one)
+    x = (x_send, x_recv, x_ssem, x_rsem, rows)
+    p = (p_send, p_recv, p_ssem, p_rsem, rows)
+
+    start(ask)
+
     row_copy.wait()
-    obs_row = jnp.where(live, row_ref[...], -1)
+    index = iota((1, slots), 1)
+    high = lax.div(index, 32)
+    fields = iota((CAP, slots), 0)
+    fields = jnp.where(
+        fields == 0,
+        high,
+        jnp.where(fields == 1, index - high * 32, jnp.where(fields == 2, row_ref[...] + 1, 0)),
+    )
+    moved = nt(fields.astype(F32).astype(BF16), one_hot(iota((places, slots), 0) == place))
+    slot_row[...] = (moved[0:1] * 32.0 + moved[1:2]).astype(I32)
+    slot_copy = pltpu.make_async_copy(slot_row, slot_at, slot_sem)
+    slot_copy.start()
+    obs_row = moved[2:3].astype(I32)
     obs_column = to_column(obs_row)
+    to_obs = one_hot(obs_row == iota((obs_blocks, places), 0) + 1)
+    from_obs = one_hot(obs_column == iota((places, obs_blocks), 1) + 1)
     emission_copy.wait()
-    ask_wait()
+    wait_recv(ask)
 
     total = jnp.sum(ask_recv[...], axis=0).astype(I32)
     picked = nn(one_hot(to_column(total) == iota((places, panel), 1) + 1), emission[...])
     x_send[...] = picked.astype(BF16)
     x_recv[own] = x_send[own]
-    x_start()
+    start(x)
 
     for copy in foot_copies:
         copy.wait()
     observed_copy.wait()
     weight_copy.wait()
     valid_copy.wait()
-    x_wait()
-
-    state[...] = nn(to_slot, x_recv[...])
-
-    sub = iota((GROUP, width), 0)
-
-    @pl.loop(0, slots // GROUP, unroll=32)
-    def _(g):
-        at = pl.ds(pl.multiple_of(g * GROUP, GROUP), GROUP)
-        blocks = foot[at].reshape(GROUP * width, width)
-        product = nt(state[at].astype(BF16), blocks)
-        out = jnp.zeros((GROUP, width), F32)
-        for k in range(GROUP):
-            out = jnp.where(sub == k, product[:, k * width : (k + 1) * width], out)
-        image_rows[at] = out
-
-    to_obs = one_hot(obs_row == iota((obs_blocks, slots), 0))
+    slot_copy.wait()
+
+    sub = iota((CAP, width), 0)
+
+    def blocks_of(panel_index):
+        first = panel_index * CAP
+        indices = [jnp.clip(slot_at[0, first + k], 0, slots - 1) for k in range(CAP)]
+        return jnp.concatenate([foot[index] for index in indices], axis=0)
+
+    for d0 in range(0, n, BATCH):
+        steps = range(d0, min(d0 + BATCH, n))
+        for d in steps:
+            if d > 0:
+                copy_from(x, d).wait_recv()
+        for d in steps:
+            source = lax.rem(me - d + n, n)
+            product = nt(x_recv[span(source)], blocks_of(source))
+            out = jnp.zeros((CAP, width), F32)
+            for k in range(CAP):
+                out = jnp.where(sub == k, product[:, k * width : (k + 1) * width], out)
+            image_rows[span(source)] = out
+
     rows_value = image_rows[...]
     high, low = split(rows_value)
     image = nn(to_obs, high) + nn(to_obs, low)
     obs_slot = iota((obs_blocks, width), 0) * width + iota((obs_blocks, width), 1)
     misfit = jnp.where(obs_slot < valid_ref[0], weight[...] * (image - observed[...]), 0.0)
     weighted_ref[...] = misfit
-    residual[...] = nn(one_hot(obs_column == iota((slots, obs_blocks), 1)), misfit.astype(BF16))
-
-    @pl.loop(0, slots // GROUP, unroll=32)
-    def _(g):
-        at = pl.ds(pl.multiple_of(g * GROUP, GROUP), GROUP)
-        blocks = foot[at].reshape(GROUP * width, width)
-        value = residual[at]
-        spread_out = jnp.concatenate(
-            [jnp.where(sub == k, value, 0.0) for k in range(GROUP)], axis=1
-        ).astype(BF16)
-        partial[at] = nn(spread_out, blocks)
-
-    high, low = split(partial[...])
-    to_place = one_hot(iota((places, slots), 0) == place)
-    p_send[:, :width] = nn(to_place, high).astype(BF16)
-    p_send[:, width:] = nn(to_place, low).astype(BF16)
-    p_recv[own] = p_send[own]
-    p_start()
+    residual[...] = nn(from_obs, misfit.astype(BF16)).astype(BF16)
+
+    for d0 in range(1, n + 1, BATCH):
+        steps = range(d0, min(d0 + BATCH, n + 1))
+        for d in steps:
+            target = lax.rem(me + d, n)
+            value = residual[span(target)].astype(F32)
+            wide = jnp.concatenate(
+                [jnp.where(sub == k, value, 0.0) for k in range(CAP)], axis=1
+            ).astype(BF16)
+            high, low = split(nn(wide, blocks_of(target)))
+            sink = p_send if d < n else p_recv
+            sink[span(target), :width] = high
+            sink[span(target), width:] = low
+        for d in steps:
+            if d < n:
+                copy_to(p, d).start()
     scatter = one_hot(iota((panel, places), 0) + 1 == total)
     prior_copy.wait()
-    ask_done()
-    x_done()
-    p_wait()
+    wait_send(ask)
+    wait_send(x)
+    wait_recv(p)
     summed = nn(scatter, p_recv[...])
     gradient_ref[...] = (
         summed[:, :width] + summed[:, width:] + prior[...] * emission[...].astype(F32)
     )
-    p_done()
+    wait_send(p)
 
 
 def in_hbm(value):
@@ -331,11 +350,12 @@
             pltpu.VMEM((places, width), BF16),
             pltpu.VMEM((places, 2 * width), BF16),
             pltpu.VMEM((places, 2 * width), BF16),
-            pltpu.VMEM((slots, width), F32),
-            pltpu.VMEM((slots, width), F32),
-            pltpu.VMEM((slots, width), F32),
-            pltpu.VMEM((slots, width), F32),
+            pltpu.VMEM((1, places), I32),
+            pltpu.SMEM((1, places), I32),
+            pltpu.VMEM((places, width), F32),
+            pltpu.VMEM((places, width), BF16),
             dma((CHUNKS,)),
+            dma(()),
             dma((8,)),
             dma((n,)),
             dma((n,)),

time: 27.3 us -> 25.8 us (0.945)
  Pallas kernels: 23.8 us -> 22.3 us
    pallas_call x1, Pallas kernels: 23.8 us -> 22.3 us  [on_device(): pl.pallas_call(functools.partial(kernel, n), out_shape=outs, in_specs=[hb...]
where the time goes in v3:
time: 25.8 us; the launch traced here: 25.7 us
  Pallas kernels  22.3 us (86%)
  between operations  1.93 us (7%)
  local copies, waits for them, and re-layouts  1.41 us (5%)
    pallas_call x1, Pallas kernels, on_device(): pl.pallas_call(functools.partial(kernel, n), out_shape=outs, in_specs=[hb...  22.3 us
    unnamed x2, local copies, waits for them, and re-layouts  1.41 us

profile of v3, /device:TPU:0, one launch (start us, length us, event | category | flops | bytes accessed | tf_op | source)
XLA Modules:
  0.0 25.7 jit_solution(14985265056026020789)
XLA Ops:
  1.9 22.3 %shard_map.104 = (f32[1024,128]{1,0:T(8,128)S(1)}, f32[64,128]{1,0:T(8,128)S(1)}) custom-call(bf16[256,128,128]{2,1,0:T(8,128)(2,1)} %foot_hbm.1, s32[1,256]{1,0:T(1,128)} %row_hbm.1, s32[1,256]{1,0:T(1,128)} %col_hbm.1, s32[1]{0:T(128)S(6)} %copy.13.count_hbm, s32[1]{0:T(128)S(6)} %copy.14.valid_hbm, bf16[1024,128]{1,0:T(8,128)(2,1)} %emission_hbm.1, ...), custom_call_target="tpu_custom_call" | custom-call | flops 16777216 | bytes 9699328 | tf_op jit(solution)/shard_map/pallas_call | solution.py:332
  24.3 0.8 %copy.15 = f32[1024,128]{1,0:T(8,128)} copy(f32[1024,128]{1,0:T(8,128)S(1)} %get-tuple-element.4) | data formatting | bytes 1048576
  25.1 0.6 %copy.16 = f32[64,128]{1,0:T(8,128)} copy(f32[64,128]{1,0:T(8,128)S(1)} %get-tuple-element.5) | data formatting | bytes 65536

commit v4 on v3

--- a/solution.py
+++ b/solution.py
@@ -9,6 +9,7 @@
 
 CAP = 16
 BATCH = 4
+PARTS = 4
 CHUNKS = 8
 MESH = pl.DeviceIdType.MESH
 BF16 = jnp.bfloat16
@@ -231,13 +232,25 @@
     to_obs = one_hot(obs_row == iota((obs_blocks, places), 0) + 1)
     from_obs = one_hot(obs_column == iota((places, obs_blocks), 1) + 1)
     emission_copy.wait()
-    wait_recv(ask)
-
-    total = jnp.sum(ask_recv[...], axis=0).astype(I32)
-    picked = nn(one_hot(to_column(total) == iota((places, panel), 1) + 1), emission[...])
-    x_send[...] = picked.astype(BF16)
-    x_recv[own] = x_send[own]
-    start(x)
+    total = jnp.zeros((1, places), I32)
+    for part in range(PARTS):
+        steps = range(part * n // PARTS, (part + 1) * n // PARTS)
+        heard = jnp.zeros((1, places), F32)
+        for d in steps:
+            if d > 0:
+                copy_from(ask, d).wait_recv()
+        for d in steps:
+            heard = heard + ask_recv[lax.rem(me - d + n, n)]
+        heard = heard.astype(I32)
+        total = total + heard
+        picked = nn(one_hot(to_column(heard) == iota((places, panel), 1) + 1), emission[...])
+        answers = x_send.at[pl.ds(part * places, places)]
+        answers[...] = picked.astype(BF16)
+        for d in steps:
+            if d > 0:
+                copy_to((answers, x_recv, x_ssem, x_rsem, rows), n - d).start()
+            else:
+                x_recv[own] = answers[own]
 
     for copy in foot_copies:
         copy.wait()
@@ -257,9 +270,9 @@
         steps = range(d0, min(d0 + BATCH, n))
         for d in steps:
             if d > 0:
-                copy_from(x, d).wait_recv()
-        for d in steps:
-            source = lax.rem(me - d + n, n)
+                copy_from(x, n - d).wait_recv()
+        for d in steps:
+            source = lax.rem(me + d, n)
             product = nt(x_recv[span(source)], blocks_of(source))
             out = jnp.zeros((CAP, width), F32)
             for k in range(CAP):
@@ -346,7 +359,7 @@
             pltpu.VMEM((panel, width), F32),
             pltpu.VMEM((n, 1, places), F32),
             pltpu.VMEM((n, 1, places), F32),
-            pltpu.VMEM((places, width), BF16),
+            pltpu.VMEM((PARTS * places, width), BF16),
             pltpu.VMEM((places, width), BF16),
             pltpu.VMEM((places, 2 * width), BF16),
             pltpu.VMEM((places, 2 * width), BF16),

time: 25.8 us -> 25.6 us (level)
    pallas_call x1, Pallas kernels: 22.3 us -> 22.1 us  [on_device(): pl.pallas_call(functools.partial(kernel, n), out_shape=outs, in_specs=[hb...]
where the time goes in v4:
time: 25.6 us; the launch traced here: 25.4 us
  Pallas kernels  22.1 us (86%)
  between operations  1.93 us (8%)
  local copies, waits for them, and re-layouts  1.41 us (6%)
    pallas_call x1, Pallas kernels, on_device(): pl.pallas_call(functools.partial(kernel, n), out_shape=outs, in_specs=[hb...  22.1 us
    unnamed x2, local copies, waits for them, and re-layouts  1.41 us

profile of v4, /device:TPU:0, one launch (start us, length us, event | category | flops | bytes accessed | tf_op | source)
XLA Modules:
  0.0 25.4 jit_solution(17992979563913287825)
XLA Ops:
  1.9 22.1 %shard_map.104 = (f32[1024,128]{1,0:T(8,128)S(1)}, f32[64,128]{1,0:T(8,128)S(1)}) custom-call(bf16[256,128,128]{2,1,0:T(8,128)(2,1)} %foot_hbm.1, s32[1,256]{1,0:T(1,128)} %row_hbm.1, s32[1,256]{1,0:T(1,128)} %col_hbm.1, s32[1]{0:T(128)S(6)} %copy.13.count_hbm, s32[1]{0:T(128)S(6)} %copy.14.valid_hbm, bf16[1024,128]{1,0:T(8,128)(2,1)} %emission_hbm.1, ...), custom_call_target="tpu_custom_call" | custom-call | flops 16777216 | bytes 9699328 | tf_op jit(solution)/shard_map/pallas_call | solution.py:345
  24.0 0.8 %copy.15 = f32[1024,128]{1,0:T(8,128)} copy(f32[1024,128]{1,0:T(8,128)S(1)} %get-tuple-element.4) | data formatting | bytes 1048576
  24.8 0.6 %copy.16 = f32[64,128]{1,0:T(8,128)} copy(f32[64,128]{1,0:T(8,128)S(1)} %get-tuple-element.5) | data formatting | bytes 65536
